TPU v7x, 256 devices: a whole 4x4x8 slice. The times are simulated.
256 devices in a mesh: rows: 32 (over z, y), feat: 8 (over x, core).
Axes of the slice: x: 4, y: 4, z: 8, core: 2. Of those that a mesh axis runs over, the one named last changes fastest.
Arguments:
- tokens: bfloat16 [20480, 5120], P('rows', 'feat'), may hold values from -6 to 6
- cotangent: bfloat16 [20480, 2048], P('rows', 'feat'), may hold values from -1.5 to 1.5
- frozen_weight: bfloat16 [5120, 2048], P('feat', 'rows'), may hold values from -0.078125 to 0.078125
- adapter_down_weight: bfloat16 [128, 32, 5120], P('rows', None, 'feat'), may hold values from -0.078125 to 0.078125
- adapter_up_weight: bfloat16 [128, 32, 2048], P('rows', None, 'feat'), may hold values from -1 to 1
- sequence_first_rows: int32 [64], replicated, may hold values from 0 to 20479, as said below
- embodiment: int32 [64], replicated, may hold values from 0 to 127
- adapter_store_row: int32 [128], replicated, may hold values from 0 to 127, each once
Outputs:
- key_value_output: bfloat16 [20480, 2048], P('rows', 'feat')
- token_gradient: bfloat16 [20480, 5120], P('rows', 'feat')
- grad_down: float32 [128, 32, 5120], P('rows', None, 'feat')
- grad_up: float32 [128, 32, 2048], P('rows', None, 'feat')
Inputs may be any that keep to these rules, and one draw needn't show every extreme that they name: sequence_first_rows[0] is 0, the values rise strictly, each block of 640 consecutive rows (rows b * 640 to (b + 1) * 640 - 1) holds exactly 2 of them, and the last one is 20479; sequence j holds the rows from sequence_first_rows[j] up to the next start.
All inputs are finite; a program needn't handle non-finite values.
Results may differ from a plain program's by a relative error of at most 0.023.
Values may be sent and summed in bfloat16 or wider, within the bound.
No kernel may reach another device: no remote copies, remote signals or barrier semaphores. Data moves between devices by JAX's collectives and lax.ppermute only.
A program may use at most 128 MiB of HBM per device.

v0:
```python
import jax
import jax.numpy as jnp
from jax import lax
from jax.experimental import pallas as pl
from jax.experimental.pallas import tpu as pltpu
from jax.sharding import Mesh
from jax.sharding import PartitionSpec as P

NZ, NY, NX, NC = 8, 4, 4, 2
RANK = 32
OWNED = 4
SLOTS = 3
SCALE = 0.5
VM = pl.BlockSpec(memory_space=pltpu.VMEM)
SM = pl.BlockSpec(memory_space=pltpu.SMEM)
ANY = pl.BlockSpec(memory_space=pl.ANY)
HB = pl.BlockSpec(memory_space=pltpu.HBM)
BF = jnp.bfloat16
F32 = jnp.float32


def near(value):
    return pltpu.with_memory_space_constraint(value, pltpu.VMEM)


def far(value):
    return pltpu.with_memory_space_constraint(value, pltpu.HBM)


def made(*shape):
    return pltpu.VMEM(shape, BF)


def made_far(*shape):
    return pltpu.HBM(shape, BF)


def copy_all(pairs, sems):
    copies = [pltpu.make_async_copy(source, target, sems.at[n]) for n, (source, target) in enumerate(pairs)]
    for copy in copies:
        copy.start()
    for copy in copies:
        copy.wait()


def params(mib):
    return pltpu.CompilerParams(vmem_limit_bytes=mib * 1024 * 1024)


def cost(flops, moved):
    return pl.CostEstimate(flops=flops, bytes_accessed=moved, transcendentals=0)


def nt(a, b):
    return lax.dot_general(a, b, (((1,), (1,)), ((), ())), preferred_element_type=F32)


def nn(a, b):
    return lax.dot_general(a, b, (((1,), (0,)), ((), ())), preferred_element_type=F32)


def tn(a, b):
    return lax.dot_general(a, b, (((0,), (0,)), ((), ())), preferred_element_type=F32)


def slot_mask(cut_ref, k, amount):
    row = lax.broadcasted_iota(jnp.int32, (1, amount), 1)
    first, second = cut_ref[0], cut_ref[1]
    if k == 0:
        return row < first
    if k == 1:
        return (row >= first) & (row < second)
    return row >= second


def shift_matrix(yi, amount):
    i = lax.broadcasted_iota(jnp.int32, (amount, amount), 0)
    j = lax.broadcasted_iota(jnp.int32, (amount, amount), 1)
    at = j + yi * (amount // NY)
    at = jnp.where(at >= amount, at - amount, at)
    return (i == at).astype(F32).astype(BF)


def pack_kernel(wt_ref, down_ref, up_ref, out_ref, sems):
    copy_all(
        (
            (wt_ref, out_ref.at[0:64]),
            (down_ref, out_ref.at[64:192]),
            (up_ref.at[0:64], out_ref.at[192:256, 0:256]),
            (up_ref.at[64:128], out_ref.at[192:256, 256:512]),
            (up_ref.at[0:64, 0:128], out_ref.at[192:256, 512:640]),
        ),
        sems,
    )


def turn_kernel(yi_ref, _1, cot_ref, out_ref):
    out_ref[...] = nn(cot_ref[...], shift_matrix(yi_ref[0], cot_ref.shape[1])).astype(BF)


def gather_pieces(all_ref, own, f, b, first):
    for k, piece in enumerate((own, *b, *f[::-1])):
        all_ref[k] = piece[first:]


def pick_kernel(at_ref, own, f1, f2, f3, f4, b1, b2, b3, *refs):
    o0, o1, o2, o3, w_ref, *_, g_ref = refs[NX:]
    gather_pieces(g_ref, own, (f1, f2, f3, f4), (b1, b2, b3), 64)
    for k, piece in enumerate((own, b1, b2, b3, f4, f3, f2, f1)):
        w_ref[k] = piece[:64]
    outs = (o0, o1, o2, o3)
    for k in range(NY):
        for s in range(SLOTS):
            at = at_ref[k * SLOTS + s]
            here = at >= 0
            at = jnp.maximum(at, 0)
            zo, a = at // OWNED, at % OWNED
            down = g_ref[zo, pl.ds(pl.multiple_of(a * RANK, RANK), RANK), :]
            up = g_ref[zo, pl.ds(pl.multiple_of(128 + (a % 2) * RANK, RANK), RANK), :]
            up = jnp.where(a >= 2, up[:, 256:512], up[:, 0:256])
            rows = slice(s * RANK, (s + 1) * RANK)
            outs[k][rows, 0:640] = jnp.where(here, down, jnp.zeros_like(down))
            outs[k][rows, 640:896] = jnp.where(here, up, jnp.zeros_like(up))


def low_kernel(cut_ref, a0, a1, a2, a3, tok_ref, cot_ref, part_ref, slots_ref):
    slots = (a0[...] + a1[...]) + (a2[...] + a3[...])
    slots_ref[...] = slots
    amount = tok_ref.shape[0]
    low = nt(slots[:, :640], tok_ref[...])
    back = nt(slots[:, 640:], cot_ref[...])
    low_sum = jnp.zeros((RANK, amount), F32)
    back_sum = jnp.zeros((RANK, amount), F32)
    for k in range(SLOTS):
        keep = slot_mask(cut_ref, k, amount)
        low_sum += jnp.where(keep, low[k * RANK:(k + 1) * RANK], 0.0)
        back_sum += jnp.where(keep, back[k * RANK:(k + 1) * RANK], 0.0)
    part_ref[0:RANK] = low_sum.astype(BF)
    part_ref[RANK:] = back_sum.astype(BF)


def term_kernel(cut_ref, p0, p1, p2, p3, tok_ref, cot_ref, term_ref, low_ref, back_ref):
    total = (p0[...].astype(F32) + p1[...].astype(F32)) + (p2[...].astype(F32) + p3[...].astype(F32))
    amount = tok_ref.shape[0]
    low, back = total[:RANK], total[RANK:]
    for k in range(SLOTS):
        keep = slot_mask(cut_ref, k, amount)
        low_ref[k * RANK:(k + 1) * RANK] = jnp.where(keep, low, 0.0).astype(BF)
        back_ref[k * RANK:(k + 1) * RANK] = jnp.where(keep, back, 0.0).astype(BF)
    term_ref[:, :640] = (SCALE * nn(back_ref[...], tok_ref[...])).astype(BF)
    term_ref[:, 640:] = (SCALE * nn(low_ref[...], cot_ref[...])).astype(BF)


def pass_kernel(*_):
    pass


def forward_kernel(_1, prev_ref, next_ref, c0, c1, c2, c3, prev_half, next_half, *refs):
    *_, buf_ref, sems = refs
    half = NZ // 2
    copy_all(((prev_ref.at[:half], buf_ref.at[0]), (next_ref.at[half:], buf_ref.at[1])), sems)
    copy_all(((buf_ref.at[0], prev_half), (buf_ref.at[1], next_half)), sems)


def load_weight(refs, w_ref, sems):
    half = NZ // 2
    own, ahead_1, far_low, far_high, behind_1 = refs
    copies = []
    for n, (ref, z, y) in enumerate(
        ((own, slice(0, NZ), 0), (ahead_1, slice(0, NZ), 1), (far_low, slice(0, half), 2), (far_high, slice(half, NZ), 2), (behind_1, slice(0, NZ), 3))
    ):
        copies.append(pltpu.make_async_copy(ref, w_ref.at[z, y * 64:(y + 1) * 64], sems.at[n]))
    for copy in copies:
        copy.start()
    return copies


def load_slices(refs, at_ref, first, w_ref, sems, start):
    half = NZ // 2
    own, ahead_1, far_low, far_high, behind_1 = refs

    def move(ref, z, k, y):
        copy = pltpu.make_async_copy(ref.at[z], w_ref.at[k, y * 64:(y + 1) * 64], sems.at[k, y])
        if start:
            copy.start()
        else:
            copy.wait()

    for k in range(NX):
        at = at_ref[first + k]
        for y, ref in ((0, own), (1, ahead_1), (3, behind_1)):
            move(ref, at, k, y)

        @pl.when(at < half)
        def _(k=k, at=at):
            move(far_low, at, k, 2)

        @pl.when(at >= half)
        def _(k=k, at=at):
            move(far_high, at - half, k, 2)


def wait_all(copies):
    for copy in copies:
        copy.wait()


def kv_send_kernel(at_ref, *refs):
    tok_ref, _, _, out_ref, w_ref, sems = refs[5:]
    load_slices(refs[:5], at_ref, NX, w_ref, sems, True)
    load_slices(refs[:5], at_ref, NX, w_ref, sems, False)

    def step(k, carry):
        out_ref[k] = nt(tok_ref[...], w_ref[k]).astype(BF)
        return carry

    lax.fori_loop(0, NX, step, 0)


def kv_keep_kernel(at_ref, *refs):
    tok_ref, other_ref, *outs, w_ref, sems = refs[5:]
    load_slices(refs[:5], at_ref, 0, w_ref, sems, True)
    load_slices(refs[:5], at_ref, 0, w_ref, sems, False)
    for k, out_ref in enumerate(outs):
        base = nt(tok_ref[...], w_ref[k])
        out_ref[...] = (base + other_ref[k].astype(F32)).astype(BF)


def kv_out_kernel(yi_ref, p0, p1, p2, p3, low_ref, slots_ref, out_ref):
    shift = shift_matrix(yi_ref[0], out_ref.shape[1])
    up = nn(slots_ref[:, 640:], shift).astype(BF)
    total = (p0[...].astype(F32) + p1[...].astype(F32)) + (p2[...].astype(F32) + p3[...].astype(F32))
    total = (total + SCALE * tn(low_ref[...], up)).astype(BF)
    out_ref[...] = nt(total, shift).astype(BF)


def input_grad_kernel(at_ref, *refs):
    cots = refs[5:5 + 2 * NX]
    back_ref, slots_ref, out_ref, acc_ref, w_ref, sems = refs[5 + 2 * NX:]
    copies = load_weight(refs[:5], w_ref, sems)
    acc_ref[...] = SCALE * tn(back_ref[...], slots_ref[:, :640])
    wait_all(copies)
    for k in range(NX):
        acc_ref[...] += nn(cots[k][...], w_ref[at_ref[k]]) + nn(cots[NX + k][...], w_ref[at_ref[NX + k]])
    out_ref[...] = acc_ref[...].astype(BF)


def bin_kernel(to_ref, own, f1, f2, f3, f4, b1, b2, b3, _1, o0, o1, o2, o3, t_ref, acc_ref):
    gather_pieces(t_ref, own, (f1, f2, f3, f4), (b1, b2, b3), 0)
    acc_ref[...] = jnp.zeros_like(acc_ref)
    for j in range(NZ * SLOTS):
        to = to_ref[j]

        @pl.when(to >= 0)
        def _(j=j, to=to):
            zs, s = j // SLOTS, j % SLOTS
            acc_ref[to] += t_ref[zs, s * RANK:(s + 1) * RANK, :].astype(F32)

    for k, o in enumerate((o0, o1, o2, o3)):
        for a in range(OWNED):
            o[a * RANK:(a + 1) * RANK] = acc_ref[k * OWNED + a].astype(BF)


def total_kernel(*refs):
    *parts, down_ref, up_ref = refs
    p0, p1, p2, p3 = (part[...].astype(F32) for part in parts)
    total = (p0 + p1) + (p2 + p3)
    down_ref[...] = total[:, :640]
    up_ref[...] = total[:, 640:]


def others(axis, n, move, values):
    return [values[0]] + [move(values[k], axis, n, k) for k in range(1, n)]


def ahead(value, axis, n, k):
    return lax.ppermute(value, axis, [(i, (i - k) % n) for i in range(n)])


def deliver(value, axis, n, k):
    return lax.ppermute(value, axis, [(i, (i + k) % n) for i in range(n)])


def ring(value):
    f, b = [value], [value]
    for _ in range(NZ // 2 - 1):
        f.append(deliver(f[-1], "z", NZ, 1))
        b.append(deliver(b[-1], "z", NZ, -1))
    f.append(deliver(f[-1], "z", NZ, 1))
    return f[1:] + b[1:]


def on_device(tokens, cot, w, down, up, first_rows, embodiment, store_row):
    zi, yi = lax.axis_index("z"), lax.axis_index("y")
    xi, ci = lax.axis_index("x"), lax.axis_index("c")
    rows, dl = tokens.shape
    cl = cot.shape[1]
    block = zi * NY + yi
    width = dl + cl

    yv = jnp.reshape(yi, (1,)).astype(jnp.int32)
    pack = pl.pallas_call(
        pack_kernel,
        out_shape=made(256, dl),
        in_specs=[HB] * 3,
        out_specs=VM,
        scratch_shapes=[pltpu.SemaphoreType.DMA((5,))],
        compiler_params=params(4),
        cost_estimate=cost(0, 700_000),
    )(far(w.T), far(down.reshape(OWNED * RANK, dl)), far(up.reshape(OWNED * RANK, cl)))
    cot_moved = pl.pallas_call(
        turn_kernel,
        out_shape=made_far(rows, cl),
        in_specs=[SM, ANY, VM],
        out_specs=VM,
        compiler_params=params(4),
        cost_estimate=cost(0, 700_000),
    )(yv, pack, far(cot))
    gathered = ring(pack)
    cot_x = others("x", NX, ahead, [cot_moved] * NX)

    seq_count = first_rows.shape[0]
    emb_hit = embodiment[:, None] == jnp.arange(store_row.shape[0], dtype=jnp.int32)[None, :]
    seq_store = jnp.sum(jnp.where(emb_hit, store_row[None, :], 0), axis=1)

    def stores_of(blocks):
        seqs = (2 * blocks[:, None] - 1 + jnp.arange(SLOTS, dtype=jnp.int32)[None, :]).reshape(-1)
        hit = jnp.maximum(seqs, 0)[:, None] == jnp.arange(seq_count, dtype=jnp.int32)[None, :]
        return jnp.sum(jnp.where(hit, seq_store[None, :], 0), axis=1)

    ks = jnp.arange(NY, dtype=jnp.int32)
    plane = stores_of(zi * NY + (yi + ks) % NY)
    pick_at = jnp.where(
        (plane // OWNED) % NY == yi, ((plane // (OWNED * NY) - zi) % NZ) * OWNED + plane % OWNED, -1
    )
    line = stores_of(((zi + jnp.arange(NZ, dtype=jnp.int32)) % NZ) * NY + yi)
    bin_to = jnp.where(
        line // (OWNED * NY) == zi, (((line // OWNED) % NY - yi) % NY) * OWNED + line % OWNED, -1
    )
    cut = lax.dynamic_slice_in_dim(first_rows, 2 * block, 2) - block * rows
    home = 2 * ((xi + jnp.arange(NX, dtype=jnp.int32)) % NX)
    w_at = jnp.concatenate([home + ci, home + 1 - ci])
    w_at = ((w_at - zi) % NZ).astype(jnp.int32)

    picked = pl.pallas_call(
        pick_kernel,
        out_shape=[made(SLOTS * RANK, width)] * NY
        + [made_far(NZ, 64, dl)]
        + [made_far(rows, cl)] * NX,
        in_specs=[SM] + [VM] * 8 + [ANY] * NX,
        out_specs=[VM] * (NY + 1) + [ANY] * NX,
        input_output_aliases={9 + k: NY + 1 + k for k in range(NX)},
        scratch_shapes=[pltpu.VMEM((NZ, 192, dl), BF)],
        compiler_params=params(6),
        cost_estimate=cost(0, 9_000_000),
    )(pick_at, *map(near, (pack, *gathered)), *map(far, cot_x))
    w_own, cot_x = picked[NY], picked[NY + 1:]
    slot_parts = others("y", NY, deliver, picked)


    part, slots = pl.pallas_call(
        low_kernel,
        out_shape=[
            made(2 * RANK, rows),
            made(SLOTS * RANK, width),
        ],
        in_specs=[SM] + [VM] * 6,
        out_specs=[VM, VM],
        compiler_params=params(6),
        cost_estimate=cost(2 * rows * SLOTS * RANK * width, 3_000_000),
    )(cut, *map(near, slot_parts), tokens, cot)

    w_own = pl.pallas_call(
        pass_kernel,
        out_shape=made_far(NZ, 64, dl),
        in_specs=[VM, ANY],
        out_specs=ANY,
        input_output_aliases={1: 0},
        compiler_params=params(4),
        cost_estimate=cost(0, 1_000),
    )(near(slot_parts[1]), far(w_own))
    w_prev, w_next = deliver(w_own, "y", NY, 1), deliver(w_own, "y", NY, -1)

    part_other = lax.ppermute(part, "c", [(0, 1), (1, 0)])
    part = (part.astype(F32) + part_other.astype(F32)).astype(BF)
    parts = others("x", NX, ahead, [part] * NX)
    term, low, back = pl.pallas_call(
        term_kernel,
        out_shape=[
            made(SLOTS * RANK, width),
            made(SLOTS * RANK, rows),
            made(SLOTS * RANK, rows),
        ],
        in_specs=[SM] + [VM] * 6,
        out_specs=[VM] * 3,
        compiler_params=params(6),
        cost_estimate=cost(2 * rows * SLOTS * RANK * width, 3_000_000),
    )(cut, *map(near, parts), tokens, cot)
    terms = ring(term)
    prev_half, next_half, *cot_x = pl.pallas_call(
        forward_kernel,
        out_shape=[made_far(NZ // 2, 64, dl)] * 2 + [made_far(rows, cl)] * NX,
        in_specs=[ANY, HB, HB] + [ANY] * NX,
        out_specs=[HB, HB] + [ANY] * NX,
        input_output_aliases={3 + k: 2 + k for k in range(NX)},
        scratch_shapes=[pltpu.VMEM((2, NZ // 2, 64, dl), BF), pltpu.SemaphoreType.DMA((2,))],
        compiler_params=params(4),
        cost_estimate=cost(0, 1_000),
    )(term, far(w_prev), far(w_next), *map(far, cot_x))
    far_low, far_high = deliver(prev_half, "y", NY, 1), deliver(next_half, "y", NY, -1)
    ws = [far(v) for v in (w_own, w_next, far_low, far_high, w_prev)]
    cot_other = [lax.ppermute(c, "c", [(0, 1), (1, 0)]) for c in cot_x]

    half = made_far(NX, rows, cl)
    kv_cost = cost(1_000, 1_000)
    kv_send = pl.pallas_call(
        kv_send_kernel,
        out_shape=half,
        in_specs=[SM] + [HB] * 5 + [VM] * 3,
        out_specs=VM,
        scratch_shapes=[pltpu.VMEM((NX, cl, dl), BF), pltpu.SemaphoreType.DMA((NX, NY))],
        compiler_params=params(8),
        cost_estimate=kv_cost,
    )(w_at, *ws, tokens, near(terms[1][:16, :128]), near(terms[NZ // 2 + 1][:16, :128]))
    kv_other = lax.ppermute(kv_send, "c", [(0, 1), (1, 0)])
    kv_keep = pl.pallas_call(
        kv_keep_kernel,
        out_shape=[made_far(rows, cl)] * NX,
        in_specs=[SM] + [HB] * 5 + [VM] * 2,
        out_specs=[VM] * NX,
        scratch_shapes=[pltpu.VMEM((NX, cl, dl), BF), pltpu.SemaphoreType.DMA((NX, NY))],
        compiler_params=params(8),
        cost_estimate=kv_cost,
    )(w_at, *ws, tokens, far(kv_other))
    kv_parts = others("x", NX, deliver, kv_keep)

    token_gradient = pl.pallas_call(
        input_grad_kernel,
        out_shape=jax.ShapeDtypeStruct((rows, dl), BF),
        in_specs=[SM] + [HB] * 5 + [VM] * (2 * NX + 2),
        out_specs=VM,
        scratch_shapes=[
            pltpu.VMEM((rows, dl), F32),
            pltpu.VMEM((NZ, cl, dl), BF),
            pltpu.SemaphoreType.DMA((5,)),
        ],
        compiler_params=params(12),
        cost_estimate=cost(1_000, 1_000),
    )(w_at, *ws, *map(far, (*cot_x, *cot_other)), near(back), near(slots))

    key_value_output = pl.pallas_call(
        kv_out_kernel,
        out_shape=jax.ShapeDtypeStruct((rows, cl), BF),
        in_specs=[SM] + [VM] * 6,
        out_specs=VM,
        compiler_params=params(8),
        cost_estimate=cost(2 * rows * cl * 512, 2_000_000),
    )(yv, far(kv_parts[0]), *map(near, kv_parts[1:]), near(low), near(slots))

    bins = pl.pallas_call(
        bin_kernel,
        out_shape=[made(OWNED * RANK, width)] * NY,
        in_specs=[SM] + [VM] * 8 + [ANY],
        out_specs=[VM] * NY,
        scratch_shapes=[pltpu.VMEM((NZ, SLOTS * RANK, width), BF), pltpu.VMEM((NY * OWNED, RANK, width), F32)],
        compiler_params=params(8),
        cost_estimate=cost(0, 1_000),
    )(bin_to, *map(near, (term, *terms)), far(kv_keep[0]))
    bin_parts = others("y", NY, deliver, bins)
    grad_down, grad_up = pl.pallas_call(
        total_kernel,
        out_shape=[
            jax.ShapeDtypeStruct((OWNED * RANK, dl), F32),
            jax.ShapeDtypeStruct((OWNED * RANK, cl), F32),
        ],
        in_specs=[VM] * NY,
        out_specs=[VM, VM],
        compiler_params=params(8),
        cost_estimate=cost(0, 2_000_000),
    )(*map(near, bin_parts))
    return (
        key_value_output,
        token_gradient,
        grad_down.reshape(OWNED, RANK, dl),
        grad_up.reshape(OWNED, RANK, cl),
    )


def solution(mesh):
    fine = Mesh(mesh.devices.reshape(NZ, NY, NX, NC), ("z", "y", "x", "c"))
    rows, feat = ("z", "y"), ("x", "c")
    return jax.shard_map(
        on_device,
        mesh=fine,
        in_specs=(
            P(rows, feat),
            P(rows, feat),
            P(feat, rows),
            P(rows, None, feat),
            P(rows, None, feat),
            P(),
            P(),
            P(),
        ),
        out_specs=(
            P(rows, feat),
            P(rows, feat),
            P(rows, None, feat),
            P(rows, None, feat),
        ),
        check_vma=False,
    )
```

profile of v0, /device:TPU:2, one launch (start us, length us, event | category | flops | bytes accessed | tf_op | source)
XLA Modules:
  0.0 131.2 jit_solution(14648781895254425287)
XLA Ops:
  3.7 4.0 %collective-permute-start.4 = (bf16[256,640]{1,0:T(8,128)(2,1)S(1)}, bf16[256,640]{1,0:T(8,128)(2,1)S(1)}, u32[]{:S(2)}, u32[]{:S(2)}) collective-permute-start(bf16[256,640]{1,0:T(8,128)(2,1)S(1)} %shard_map.111._1.own), channel_id=1, source_target_pairs={{0,224},{32,0},{64,32},{96,64},{128,96},{160,128},{192,160},{224,1... | collective-permute-start | bytes 983048 | tf_op jit(solution)/shard_map/ppermute | solution.py:281
  7.7 7.6 %collective-permute-done.f1 = bf16[256,640]{1,0:T(8,128)(2,1)S(1)} collective-permute-done((bf16[256,640]{1,0:T(8,128)(2,1)S(1)}, bf16[256,640]{1,0:T(8,128)(2,1)S(1)}, u32[]{:S(2)}, u32[]{:S(2)}) %collective-permute-start) | collective-permute-done | bytes 327712 | tf_op jit(solution)/shard_map/ppermute | solution.py:281
  19.9 2.2 %collective-permute-start.7 = (bf16[640,256]{1,0:T(8,128)(2,1)}, bf16[640,256]{1,0:T(8,128)(2,1)S(1)}, u32[]{:S(2)}, u32[]{:S(2)}) collective-permute-start(bf16[640,256]{1,0:T(8,128)(2,1)} %shard_map.112.refs_0_), channel_id=1, source_target_pairs={{0,6},{2,0},{4,2},{6,4},{1,7},{3,1},{5,3},{7,5},{8,14},{10,8},{12,... | collective-permute-start | bytes 983048 | tf_op jit(solution)/shard_map/ppermute | solution.py:277
  22.0 3.3 %collective-permute-start.5 = (bf16[256,640]{1,0:T(8,128)(2,1)S(1)}, bf16[256,640]{1,0:T(8,128)(2,1)S(1)}, u32[]{:S(2)}, u32[]{:S(2)}) collective-permute-start(bf16[256,640]{1,0:T(8,128)(2,1)S(1)} %collective-permute-done.4.b1), channel_id=1, source_target_pairs={{0,224},{32,0},{64,32},{96,64},{128,96},{160,128},{192,160},{224,1... | collective-permute-start | bytes 983048 | tf_op jit(solution)/shard_map/ppermute | solution.py:281
  25.8 4.9 %collective-permute-done.5.b2 = bf16[256,640]{1,0:T(8,128)(2,1)S(1)} collective-permute-done((bf16[256,640]{1,0:T(8,128)(2,1)S(1)}, bf16[256,640]{1,0:T(8,128)(2,1)S(1)}, u32[]{:S(2)}, u32[]{:S(2)}) %collective-permute-start.5) | collective-permute-done | bytes 327712 | tf_op jit(solution)/shard_map/ppermute | solution.py:281
  30.7 3.7 %collective-permute-start.6 = (bf16[256,640]{1,0:T(8,128)(2,1)S(1)}, bf16[256,640]{1,0:T(8,128)(2,1)S(1)}, u32[]{:S(2)}, u32[]{:S(2)}) collective-permute-start(bf16[256,640]{1,0:T(8,128)(2,1)S(1)} %collective-permute-done.5.b2), channel_id=1, source_target_pairs={{0,224},{32,0},{64,32},{96,64},{128,96},{160,128},{192,160},{224,1... | collective-permute-start | bytes 983048 | tf_op jit(solution)/shard_map/ppermute | solution.py:281
  35.4 3.5 %collective-permute-done.6.b3 = bf16[256,640]{1,0:T(8,128)(2,1)S(1)} collective-permute-done((bf16[256,640]{1,0:T(8,128)(2,1)S(1)}, bf16[256,640]{1,0:T(8,128)(2,1)S(1)}, u32[]{:S(2)}, u32[]{:S(2)}) %collective-permute-start.6) | collective-permute-done | bytes 327712 | tf_op jit(solution)/shard_map/ppermute | solution.py:281
  38.9 4.0 %collective-permute-done.3.f4 = bf16[256,640]{1,0:T(8,128)(2,1)S(1)} collective-permute-done((bf16[256,640]{1,0:T(8,128)(2,1)S(1)}, bf16[256,640]{1,0:T(8,128)(2,1)S(1)}, u32[]{:S(2)}, u32[]{:S(2)}) %collective-permute-start.3) | collective-permute-done | bytes 327712 | tf_op jit(solution)/shard_map/ppermute | solution.py:281
  46.2 2.9 %collective-permute-start.12 = (bf16[96,896]{1,0:T(8,128)(2,1)S(1)}, bf16[96,896]{1,0:T(8,128)(2,1)S(1)}, u32[]{:S(2)}, u32[]{:S(2)}) collective-permute-start(bf16[96,896]{1,0:T(8,128)(2,1)S(1)} %get-tuple-element.37), channel_id=1, source_target_pairs={{0,16},{8,24},{16,0},{24,8},{1,17},{9,25},{17,1},{25,9},{2,18},{10... | collective-permute-start | bytes 516104 | tf_op jit(solution)/shard_map/ppermute | solution.py:281
  53.4 2.3 %collective-permute-start.11 = (bf16[8,64,640]{2,1,0:T(8,128)(2,1)}, bf16[8,64,640]{2,1,0:T(8,128)(2,1)}, u32[]{:S(2)}, u32[]{:S(2)}) collective-permute-start(bf16[8,64,640]{2,1,0:T(8,128)(2,1)} %shard_map.114.refs_0_), channel_id=1, source_target_pairs={{0,24},{8,0},{16,8},{24,16},{1,25},{9,1},{17,9},{25,17},{2,26},{10... | collective-permute-start | bytes 1966088 | tf_op jit(solution)/shard_map/ppermute | solution.py:281
  55.8 2.2 %collective-permute-done.12.a2 = bf16[96,896]{1,0:T(8,128)(2,1)S(1)} collective-permute-done((bf16[96,896]{1,0:T(8,128)(2,1)S(1)}, bf16[96,896]{1,0:T(8,128)(2,1)S(1)}, u32[]{:S(2)}, u32[]{:S(2)}) %collective-permute-start.12) | collective-permute-done | bytes 172064 | tf_op jit(solution)/shard_map/ppermute | solution.py:281
  65.5 3.4 %collective-permute-done.16.p2 = bf16[64,640]{1,0:T(8,128)(2,1)S(1)} collective-permute-done((bf16[64,640]{1,0:T(8,128)(2,1)S(1)}, bf16[64,640]{1,0:T(8,128)(2,1)S(1)}, u32[]{:S(2)}, u32[]{:S(2)}) %collective-permute-start.16) | collective-permute-done | bytes 81952 | tf_op jit(solution)/shard_map/ppermute | solution.py:277
  75.5 3.2 %collective-permute-start.20 = (bf16[4,64,640]{2,1,0:T(8,128)(2,1)}, bf16[4,64,640]{2,1,0:T(8,128)(2,1)S(1)}, u32[]{:S(2)}, u32[]{:S(2)}) collective-permute-start(bf16[4,64,640]{2,1,0:T(8,128)(2,1)} %get-tuple-element.46), channel_id=1, source_target_pairs={{0,24},{8,0},{16,8},{24,16},{1,25},{9,1},{17,9},{25,17},{2,26},{10... | collective-permute-start | bytes 983048 | tf_op jit(solution)/shard_map/ppermute | solution.py:281
  80.8 3.3 %collective-permute-done.24.b2 = bf16[96,896]{1,0:T(8,128)(2,1)S(1)} collective-permute-done((bf16[96,896]{1,0:T(8,128)(2,1)S(1)}, bf16[96,896]{1,0:T(8,128)(2,1)S(1)}, u32[]{:S(2)}, u32[]{:S(2)}) %collective-permute-start.24) | collective-permute-done | bytes 172064 | tf_op jit(solution)/shard_map/ppermute | solution.py:281
  84.1 2.5 %collective-permute-done.22.f2 = bf16[96,896]{1,0:T(8,128)(2,1)S(1)} collective-permute-done((bf16[96,896]{1,0:T(8,128)(2,1)S(1)}, bf16[96,896]{1,0:T(8,128)(2,1)S(1)}, u32[]{:S(2)}, u32[]{:S(2)}) %collective-permute-start.22) | collective-permute-done | bytes 172064 | tf_op jit(solution)/shard_map/ppermute | solution.py:281
  88.1 4.9 %shard_map.118 = bf16[4,640,256]{2,1,0:T(8,128)(2,1)} custom-call(s32[8]{0:T(128)S(1)} %and_select_fusion.12.at_ref, bf16[8,64,640]{2,1,0:T(8,128)(2,1)} %shard_map.114.refs_0_, bf16[8,64,640]{2,1,0:T(8,128)(2,1)} %collective-permute-done.11.next_ref.refs_1_, bf16[4,64,640]{2,1,0:T(8,128)(2,1)} %copy-done.4, bf16[4,64,640]{2,1,0:T(8,128)(2,1)} %copy-done.5, ...), custom_call_target="tpu_custom_call" | custom-call | flops 1000 | bytes 1000 | tf_op jit(solution)/shard_map/pallas_call | solution.py:416
  96.2 3.8 %collective-permute-done.35.b3 = bf16[96,896]{1,0:T(8,128)(2,1)S(1)} collective-permute-done((bf16[96,896]{1,0:T(8,128)(2,1)S(1)}, bf16[96,896]{1,0:T(8,128)(2,1)S(1)}, u32[]{:S(2)}, u32[]{:S(2)}) %collective-permute-start.35) | collective-permute-done | bytes 172064 | tf_op jit(solution)/shard_map/ppermute | solution.py:281
  102.1 4.9 %shard_map.119 = (bf16[640,256]{1,0:T(8,128)(2,1)}, bf16[640,256]{1,0:T(8,128)(2,1)}, bf16[640,256]{1,0:T(8,128)(2,1)}, bf16[640,256]{1,0:T(8,128)(2,1)}) custom-call(s32[8]{0:T(128)S(1)} %and_select_fusion.12.at_ref, bf16[8,64,640]{2,1,0:T(8,128)(2,1)} %shard_map.114.refs_0_, bf16[8,64,640]{2,1,0:T(8,128)(2,1)} %collective-permute-done.11.next_ref.refs_1_, ...), custom_call_target="tpu_custom_call" | custom-call | flops 1000 | bytes 1000 | tf_op jit(solution)/shard_map/pallas_call | solution.py:426
  107.0 2.5 %collective-permute-done.34.f4 = bf16[96,896]{1,0:T(8,128)(2,1)S(1)} collective-permute-done((bf16[96,896]{1,0:T(8,128)(2,1)S(1)}, bf16[96,896]{1,0:T(8,128)(2,1)S(1)}, u32[]{:S(2)}, u32[]{:S(2)}) %collective-permute-start.34) | collective-permute-done | bytes 172064 | tf_op jit(solution)/shard_map/ppermute | solution.py:281
  111.4 2.3 %collective-permute-start.27 = (bf16[640,256]{1,0:T(8,128)(2,1)S(1)}, bf16[640,256]{1,0:T(8,128)(2,1)S(1)}, u32[]{:S(2)}, u32[]{:S(2)}) collective-permute-start(bf16[640,256]{1,0:T(8,128)(2,1)S(1)} %copy-done.16), channel_id=1, source_target_pairs={{0,4},{2,6},{4,0},{6,2},{1,5},{3,7},{5,1},{7,3},{8,12},{10,14},{12... | collective-permute-start | bytes 983048 | tf_op jit(solution)/shard_map/ppermute | solution.py:281
  113.7 2.2 %collective-permute-start.28 = (bf16[640,256]{1,0:T(8,128)(2,1)S(1)}, bf16[640,256]{1,0:T(8,128)(2,1)S(1)}, u32[]{:S(2)}, u32[]{:S(2)}) collective-permute-start(bf16[640,256]{1,0:T(8,128)(2,1)S(1)} %copy-done.15), channel_id=1, source_target_pairs={{0,6},{2,0},{4,2},{6,4},{1,7},{3,1},{5,3},{7,5},{8,14},{10,8},{12,... | collective-permute-start | bytes 983048 | tf_op jit(solution)/shard_map/ppermute | solution.py:281
  115.9 3.0 %collective-permute-start.37 = (bf16[128,896]{1,0:T(8,128)(2,1)S(1)}, bf16[128,896]{1,0:T(8,128)(2,1)S(1)}, u32[]{:S(2)}, u32[]{:S(2)}) collective-permute-start(bf16[128,896]{1,0:T(8,128)(2,1)S(1)} %get-tuple-element.60), channel_id=1, source_target_pairs={{0,16},{8,24},{16,0},{24,8},{1,17},{9,25},{17,1},{25,9},{2,18},{10... | collective-permute-start | bytes 688136 | tf_op jit(solution)/shard_map/ppermute | solution.py:281
  120.6 6.9 %shard_map.121 = bf16[640,640]{1,0:T(8,128)(2,1)} custom-call(s32[8]{0:T(128)S(1)} %and_select_fusion.12.at_ref, bf16[8,64,640]{2,1,0:T(8,128)(2,1)} %shard_map.114.refs_0_, bf16[8,64,640]{2,1,0:T(8,128)(2,1)} %collective-permute-done.11.next_ref.refs_1_, bf16[4,64,640]{2,1,0:T(8,128)(2,1)} %copy-done.4, bf16[4,64,640]{2,1,0:T(8,128)(2,1)} %copy-done.5, ...), custom_call_target="tpu_custom_call" | custom-call | flops 1000 | bytes 1000 | tf_op jit(solution)/shard_map/pallas_call | solution.py:437
  129.0 2.3 %shard_map.120 = bf16[640,256]{1,0:T(8,128)(2,1)} custom-call(s32[1]{0:T(128)} %bitcast.yi_ref, bf16[640,256]{1,0:T(8,128)(2,1)} %get-tuple-element.47.p0._1, bf16[640,256]{1,0:T(8,128)(2,1)S(1)} %collective-permute-done.26.p1, bf16[640,256]{1,0:T(8,128)(2,1)S(1)} %collective-permute-done.27.p2, bf16[640,256]{1,0:T(8,128)(2,1)S(1)} %collective-permute-done.28.p3, ...), custom_call_target="tpu_custom_call" | custom-call | flops 167772160 | bytes 2000000 | tf_op jit(solution)/shard_map/pallas_call | solution.py:451
  (124 shorter events, 44.6 us)
Async XLA Ops:
  1.7 13.6 %collective-permute-start = (bf16[256,640]{1,0:T(8,128)(2,1)S(1)}, bf16[256,640]{1,0:T(8,128)(2,1)S(1)}, u32[]{:S(2)}, u32[]{:S(2)}) collective-permute-start(bf16[256,640]{1,0:T(8,128)(2,1)S(1)} %shard_map.111._1.own), channel_id=1, source_target_pairs={{0,32},{32,64},{64,96},{96,128},{128,160},{160,192},{192,224},{224... | collective-permute-start | bytes 983048 | tf_op jit(solution)/shard_map/ppermute | solution.py:281
  3.7 18.4 %collective-permute-start.4 = (bf16[256,640]{1,0:T(8,128)(2,1)S(1)}, bf16[256,640]{1,0:T(8,128)(2,1)S(1)}, u32[]{:S(2)}, u32[]{:S(2)}) collective-permute-start(bf16[256,640]{1,0:T(8,128)(2,1)S(1)} %shard_map.111._1.own), channel_id=1, source_target_pairs={{0,224},{32,0},{64,32},{96,64},{128,96},{160,128},{192,160},{224,1... | collective-permute-start | bytes 983048 | tf_op jit(solution)/shard_map/ppermute | solution.py:281
  15.3 10.1 %collective-permute-start.1 = (bf16[256,640]{1,0:T(8,128)(2,1)S(1)}, bf16[256,640]{1,0:T(8,128)(2,1)S(1)}, u32[]{:S(2)}, u32[]{:S(2)}) collective-permute-start(bf16[256,640]{1,0:T(8,128)(2,1)S(1)} %collective-permute-done.f1), channel_id=1, source_target_pairs={{0,32},{32,64},{64,96},{96,128},{128,160},{160,192},{192,224},{224... | collective-permute-start | bytes 983048 | tf_op jit(solution)/shard_map/ppermute | solution.py:281
  17.3 17.6 %collective-permute-start.9 = (bf16[640,256]{1,0:T(8,128)(2,1)}, bf16[640,256]{1,0:T(8,128)(2,1)S(1)}, u32[]{:S(2)}, u32[]{:S(2)}) collective-permute-start(bf16[640,256]{1,0:T(8,128)(2,1)} %shard_map.112.refs_0_), channel_id=1, source_target_pairs={{0,2},{2,4},{4,6},{6,0},{1,3},{3,5},{5,7},{7,1},{8,10},{10,12},{12... | collective-permute-start | bytes 983048 | tf_op jit(solution)/shard_map/ppermute | solution.py:277
  18.8 16.1 %collective-permute-start.8 = (bf16[640,256]{1,0:T(8,128)(2,1)}, bf16[640,256]{1,0:T(8,128)(2,1)S(1)}, u32[]{:S(2)}, u32[]{:S(2)}) collective-permute-start(bf16[640,256]{1,0:T(8,128)(2,1)} %shard_map.112.refs_0_), channel_id=1, source_target_pairs={{0,4},{2,6},{4,0},{6,2},{1,5},{3,7},{5,1},{7,3},{8,12},{10,14},{12... | collective-permute-start | bytes 983048 | tf_op jit(solution)/shard_map/ppermute | solution.py:277
  19.9 15.6 %collective-permute-start.7 = (bf16[640,256]{1,0:T(8,128)(2,1)}, bf16[640,256]{1,0:T(8,128)(2,1)S(1)}, u32[]{:S(2)}, u32[]{:S(2)}) collective-permute-start(bf16[640,256]{1,0:T(8,128)(2,1)} %shard_map.112.refs_0_), channel_id=1, source_target_pairs={{0,6},{2,0},{4,2},{6,4},{1,7},{3,1},{5,3},{7,5},{8,14},{10,8},{12,... | collective-permute-start | bytes 983048 | tf_op jit(solution)/shard_map/ppermute | solution.py:277
  22.0 8.6 %collective-permute-start.5 = (bf16[256,640]{1,0:T(8,128)(2,1)S(1)}, bf16[256,640]{1,0:T(8,128)(2,1)S(1)}, u32[]{:S(2)}, u32[]{:S(2)}) collective-permute-start(bf16[256,640]{1,0:T(8,128)(2,1)S(1)} %collective-permute-done.4.b1), channel_id=1, source_target_pairs={{0,224},{32,0},{64,32},{96,64},{128,96},{160,128},{192,160},{224,1... | collective-permute-start | bytes 983048 | tf_op jit(solution)/shard_map/ppermute | solution.py:281
  25.4 9.2 %collective-permute-start.2 = (bf16[256,640]{1,0:T(8,128)(2,1)S(1)}, bf16[256,640]{1,0:T(8,128)(2,1)S(1)}, u32[]{:S(2)}, u32[]{:S(2)}) collective-permute-start(bf16[256,640]{1,0:T(8,128)(2,1)S(1)} %collective-permute-done.1.f2), channel_id=1, source_target_pairs={{0,32},{32,64},{64,96},{96,128},{128,160},{160,192},{192,224},{224... | collective-permute-start | bytes 983048 | tf_op jit(solution)/shard_map/ppermute | solution.py:281
  46.2 11.8 %collective-permute-start.12 = (bf16[96,896]{1,0:T(8,128)(2,1)S(1)}, bf16[96,896]{1,0:T(8,128)(2,1)S(1)}, u32[]{:S(2)}, u32[]{:S(2)}) collective-permute-start(bf16[96,896]{1,0:T(8,128)(2,1)S(1)} %get-tuple-element.37), channel_id=1, source_target_pairs={{0,16},{8,24},{16,0},{24,8},{1,17},{9,25},{17,1},{25,9},{2,18},{10... | collective-permute-start | bytes 516104 | tf_op jit(solution)/shard_map/ppermute | solution.py:281
  49.1 8.9 %collective-permute-start.13 = (bf16[96,896]{1,0:T(8,128)(2,1)S(1)}, bf16[96,896]{1,0:T(8,128)(2,1)S(1)}, u32[]{:S(2)}, u32[]{:S(2)}) collective-permute-start(bf16[96,896]{1,0:T(8,128)(2,1)S(1)} %get-tuple-element.38), channel_id=1, source_target_pairs={{0,24},{8,0},{16,8},{24,16},{1,25},{9,1},{17,9},{25,17},{2,26},{10... | collective-permute-start | bytes 516104 | tf_op jit(solution)/shard_map/ppermute | solution.py:281
  52.5 20.1 %collective-permute-start.18 = (bf16[8,64,640]{2,1,0:T(8,128)(2,1)}, bf16[8,64,640]{2,1,0:T(8,128)(2,1)S(1)}, u32[]{:S(2)}, u32[]{:S(2)}) collective-permute-start(bf16[8,64,640]{2,1,0:T(8,128)(2,1)} %shard_map.114.refs_0_), channel_id=1, source_target_pairs={{0,8},{8,16},{16,24},{24,0},{1,9},{9,17},{17,25},{25,1},{2,10},{10... | collective-permute-start | bytes 1966088 | tf_op jit(solution)/shard_map/ppermute | solution.py:281
  53.4 19.1 %collective-permute-start.11 = (bf16[8,64,640]{2,1,0:T(8,128)(2,1)}, bf16[8,64,640]{2,1,0:T(8,128)(2,1)}, u32[]{:S(2)}, u32[]{:S(2)}) collective-permute-start(bf16[8,64,640]{2,1,0:T(8,128)(2,1)} %shard_map.114.refs_0_), channel_id=1, source_target_pairs={{0,24},{8,0},{16,8},{24,16},{1,25},{9,1},{17,9},{25,17},{2,26},{10... | collective-permute-start | bytes 1966088 | tf_op jit(solution)/shard_map/ppermute | solution.py:281
  70.6 9.4 %collective-permute-start.21 = (bf16[96,896]{1,0:T(8,128)(2,1)S(1)}, bf16[96,896]{1,0:T(8,128)(2,1)S(1)}, u32[]{:S(2)}, u32[]{:S(2)}) collective-permute-start(bf16[96,896]{1,0:T(8,128)(2,1)S(1)} %get-tuple-element.40._1.own), channel_id=1, source_target_pairs={{0,32},{32,64},{64,96},{96,128},{128,160},{160,192},{192,224},{224... | collective-permute-start | bytes 516104 | tf_op jit(solution)/shard_map/ppermute | solution.py:281
  75.4 11.3 %collective-permute-start.19 = (bf16[4,64,640]{2,1,0:T(8,128)(2,1)}, bf16[4,64,640]{2,1,0:T(8,128)(2,1)S(1)}, u32[]{:S(2)}, u32[]{:S(2)}) collective-permute-start(bf16[4,64,640]{2,1,0:T(8,128)(2,1)} %get-tuple-element.45), channel_id=1, source_target_pairs={{0,8},{8,16},{16,24},{24,0},{1,9},{9,17},{17,25},{25,1},{2,10},{10... | collective-permute-start | bytes 983048 | tf_op jit(solution)/shard_map/ppermute | solution.py:281
  75.5 11.2 %collective-permute-start.20 = (bf16[4,64,640]{2,1,0:T(8,128)(2,1)}, bf16[4,64,640]{2,1,0:T(8,128)(2,1)S(1)}, u32[]{:S(2)}, u32[]{:S(2)}) collective-permute-start(bf16[4,64,640]{2,1,0:T(8,128)(2,1)} %get-tuple-element.46), channel_id=1, source_target_pairs={{0,24},{8,0},{16,8},{24,16},{1,25},{9,1},{17,9},{25,17},{2,26},{10... | collective-permute-start | bytes 983048 | tf_op jit(solution)/shard_map/ppermute | solution.py:281
  95.6 15.7 %collective-permute-start.29 = (bf16[640,256]{1,0:T(8,128)(2,1)S(1)}, bf16[640,256]{1,0:T(8,128)(2,1)S(1)}, u32[]{:S(2)}, u32[]{:S(2)}) collective-permute-start(bf16[640,256]{1,0:T(8,128)(2,1)S(1)} %copy-done.3), channel_id=1, source_target_pairs={{0,1},{1,0},{2,3},{3,2},{4,5},{5,4},{6,7},{7,6},{8,9},{9,8},{10,11... | collective-permute-start | bytes 983048 | tf_op jit(solution)/shard_map/ppermute | solution.py:412
  95.7 15.7 %collective-permute-start.30 = (bf16[640,256]{1,0:T(8,128)(2,1)}, bf16[640,256]{1,0:T(8,128)(2,1)S(1)}, u32[]{:S(2)}, u32[]{:S(2)}) collective-permute-start(bf16[640,256]{1,0:T(8,128)(2,1)} %get-tuple-element.54.refs_6_), channel_id=1, source_target_pairs={{0,1},{1,0},{2,3},{3,2},{4,5},{5,4},{6,7},{7,6},{8,9},{9,8},{10,11... | collective-permute-start | bytes 983048 | tf_op jit(solution)/shard_map/ppermute | solution.py:412
  100.0 13.7 %collective-permute-start.31 = (bf16[640,256]{1,0:T(8,128)(2,1)}, bf16[640,256]{1,0:T(8,128)(2,1)S(1)}, u32[]{:S(2)}, u32[]{:S(2)}) collective-permute-start(bf16[640,256]{1,0:T(8,128)(2,1)} %get-tuple-element.55.refs_7_), channel_id=1, source_target_pairs={{0,1},{1,0},{2,3},{3,2},{4,5},{5,4},{6,7},{7,6},{8,9},{9,8},{10,11... | collective-permute-start | bytes 983048 | tf_op jit(solution)/shard_map/ppermute | solution.py:412
  101.5 14.4 %collective-permute-start.32 = (bf16[640,256]{1,0:T(8,128)(2,1)S(1)}, bf16[640,256]{1,0:T(8,128)(2,1)S(1)}, u32[]{:S(2)}, u32[]{:S(2)}) collective-permute-start(bf16[640,256]{1,0:T(8,128)(2,1)S(1)} %copy-done.7), channel_id=1, source_target_pairs={{0,1},{1,0},{2,3},{3,2},{4,5},{5,4},{6,7},{7,6},{8,9},{9,8},{10,11... | collective-permute-start | bytes 983048 | tf_op jit(solution)/shard_map/ppermute | solution.py:412
  111.3 17.6 %collective-permute-start.26 = (bf16[640,256]{1,0:T(8,128)(2,1)S(1)}, bf16[640,256]{1,0:T(8,128)(2,1)S(1)}, u32[]{:S(2)}, u32[]{:S(2)}) collective-permute-start(bf16[640,256]{1,0:T(8,128)(2,1)S(1)} %copy-done.17), channel_id=1, source_target_pairs={{0,2},{2,4},{4,6},{6,0},{1,3},{3,5},{5,7},{7,1},{8,10},{10,12},{12... | collective-permute-start | bytes 983048 | tf_op jit(solution)/shard_map/ppermute | solution.py:281
  111.4 17.5 %collective-permute-start.27 = (bf16[640,256]{1,0:T(8,128)(2,1)S(1)}, bf16[640,256]{1,0:T(8,128)(2,1)S(1)}, u32[]{:S(2)}, u32[]{:S(2)}) collective-permute-start(bf16[640,256]{1,0:T(8,128)(2,1)S(1)} %copy-done.16), channel_id=1, source_target_pairs={{0,4},{2,6},{4,0},{6,2},{1,5},{3,7},{5,1},{7,3},{8,12},{10,14},{12... | collective-permute-start | bytes 983048 | tf_op jit(solution)/shard_map/ppermute | solution.py:281
  113.7 15.2 %collective-permute-start.28 = (bf16[640,256]{1,0:T(8,128)(2,1)S(1)}, bf16[640,256]{1,0:T(8,128)(2,1)S(1)}, u32[]{:S(2)}, u32[]{:S(2)}) collective-permute-start(bf16[640,256]{1,0:T(8,128)(2,1)S(1)} %copy-done.15), channel_id=1, source_target_pairs={{0,6},{2,0},{4,2},{6,4},{1,7},{3,1},{5,3},{7,5},{8,14},{10,8},{12,... | collective-permute-start | bytes 983048 | tf_op jit(solution)/shard_map/ppermute | solution.py:281
  115.9 11.6 %collective-permute-start.37 = (bf16[128,896]{1,0:T(8,128)(2,1)S(1)}, bf16[128,896]{1,0:T(8,128)(2,1)S(1)}, u32[]{:S(2)}, u32[]{:S(2)}) collective-permute-start(bf16[128,896]{1,0:T(8,128)(2,1)S(1)} %get-tuple-element.60), channel_id=1, source_target_pairs={{0,16},{8,24},{16,0},{24,8},{1,17},{9,25},{17,1},{25,9},{2,18},{10... | collective-permute-start | bytes 688136 | tf_op jit(solution)/shard_map/ppermute | solution.py:281
  119.1 9.0 %collective-permute-start.38 = (bf16[128,896]{1,0:T(8,128)(2,1)S(1)}, bf16[128,896]{1,0:T(8,128)(2,1)S(1)}, u32[]{:S(2)}, u32[]{:S(2)}) collective-permute-start(bf16[128,896]{1,0:T(8,128)(2,1)S(1)} %get-tuple-element.61), channel_id=1, source_target_pairs={{0,24},{8,0},{16,8},{24,16},{1,25},{9,1},{17,9},{25,17},{2,26},{10... | collective-permute-start | bytes 688136 | tf_op jit(solution)/shard_map/ppermute | solution.py:281
  (35 other events, 282.0 us)
where the time goes:
time: 132 us; the launch traced here: 131 us
  starting transfers between devices  52.5 us (40%)
  waiting for transfers between devices  44.8 us (34%)
  Pallas kernels  29.5 us (22%)
  local copies, waits for them, and re-layouts  2.54 us (2%)
    ppermute x27, starting transfers between devices, deliver(): return lax.ppermute(value, axis, [(i, (i + k) % n) for i in range(n)])  42 us
    ppermute x27, waiting for transfers between devices, deliver(): return lax.ppermute(value, axis, [(i, (i + k) % n) for i in range(n)])  38.8 us
    ppermute x6, starting transfers between devices, ahead(): return lax.ppermute(value, axis, [(i, (i - k) % n) for i in range(n)])  9.58 us
    pallas_call x1, Pallas kernels, on_device(): pl.pallas_call(input_grad_kernel, out_shape=jax.ShapeDtypeStruct((rows, d...  6.94 us
    pallas_call x1, Pallas kernels, on_device(): pl.pallas_call(kv_send_kernel, out_shape=half, in_specs=[SM] + [HB] * 5 +...  4.92 us
    pallas_call x1, Pallas kernels, on_device(): pl.pallas_call(kv_keep_kernel, out_shape=[made_far(rows, cl)] * NX, in_sp...  4.9 us
    ppermute x6, waiting for transfers between devices, ahead(): return lax.ppermute(value, axis, [(i, (i - k) % n) for i in range(n)])  4.71 us
  transfers between devices with their start and end apart: 39, of which 19 were waited for; matrix products, arithmetic and copies ran while one was open for 1% of the time, Pallas kernels for 15%

commit v1 on v0

--- a/solution.py
+++ b/solution.py
@@ -82,16 +82,14 @@
 
 
 def pack_kernel(wt_ref, down_ref, up_ref, out_ref, sems):
-    copy_all(
-        (
-            (wt_ref, out_ref.at[0:64]),
-            (down_ref, out_ref.at[64:192]),
-            (up_ref.at[0:64], out_ref.at[192:256, 0:256]),
-            (up_ref.at[64:128], out_ref.at[192:256, 256:512]),
-            (up_ref.at[0:64, 0:128], out_ref.at[192:256, 512:640]),
-        ),
-        sems,
-    )
+    pairs = []
+    for j in range(5):
+        columns = slice(j * 128, (j + 1) * 128)
+        pairs.append((wt_ref.at[:, columns], out_ref.at[j * 64:(j + 1) * 64]))
+        pairs.append((down_ref.at[:, columns], out_ref.at[320 + j * 128:448 + j * 128]))
+    for j in range(2):
+        pairs.append((up_ref.at[:, j * 128:(j + 1) * 128], out_ref.at[960 + j * 128:1088 + j * 128]))
+    copy_all(pairs, sems)
 
 
 def turn_kernel(yi_ref, _1, cot_ref, out_ref):
@@ -105,9 +103,10 @@
 
 def pick_kernel(at_ref, own, f1, f2, f3, f4, b1, b2, b3, *refs):
     o0, o1, o2, o3, w_ref, *_, g_ref = refs[NX:]
-    gather_pieces(g_ref, own, (f1, f2, f3, f4), (b1, b2, b3), 64)
+    gather_pieces(g_ref, own, (f1, f2, f3, f4), (b1, b2, b3), 320)
     for k, piece in enumerate((own, b1, b2, b3, f4, f3, f2, f1)):
-        w_ref[k] = piece[:64]
+        for j in range(5):
+            w_ref[k, :, j * 128:(j + 1) * 128] = piece[j * 64:(j + 1) * 64]
     outs = (o0, o1, o2, o3)
     for k in range(NY):
         for s in range(SLOTS):
@@ -115,12 +114,9 @@
             here = at >= 0
             at = jnp.maximum(at, 0)
             zo, a = at // OWNED, at % OWNED
-            down = g_ref[zo, pl.ds(pl.multiple_of(a * RANK, RANK), RANK), :]
-            up = g_ref[zo, pl.ds(pl.multiple_of(128 + (a % 2) * RANK, RANK), RANK), :]
-            up = jnp.where(a >= 2, up[:, 256:512], up[:, 0:256])
-            rows = slice(s * RANK, (s + 1) * RANK)
-            outs[k][rows, 0:640] = jnp.where(here, down, jnp.zeros_like(down))
-            outs[k][rows, 640:896] = jnp.where(here, up, jnp.zeros_like(up))
+            for j in range(7):
+                part = g_ref[zo, pl.ds(pl.multiple_of(j * 128 + a * RANK, RANK), RANK), :]
+                outs[k][s * RANK:(s + 1) * RANK, j * 128:(j + 1) * 128] = jnp.where(here, part, jnp.zeros_like(part))
 
 
 def low_kernel(cut_ref, a0, a1, a2, a3, tok_ref, cot_ref, part_ref, slots_ref):
@@ -301,10 +297,10 @@
     yv = jnp.reshape(yi, (1,)).astype(jnp.int32)
     pack = pl.pallas_call(
         pack_kernel,
-        out_shape=made(256, dl),
+        out_shape=made(1216, 128),
         in_specs=[HB] * 3,
         out_specs=VM,
-        scratch_shapes=[pltpu.SemaphoreType.DMA((5,))],
+        scratch_shapes=[pltpu.SemaphoreType.DMA((12,))],
         compiler_params=params(4),
         cost_estimate=cost(0, 700_000),
     )(far(w.T), far(down.reshape(OWNED * RANK, dl)), far(up.reshape(OWNED * RANK, cl)))
@@ -350,7 +346,7 @@
         in_specs=[SM] + [VM] * 8 + [ANY] * NX,
         out_specs=[VM] * (NY + 1) + [ANY] * NX,
         input_output_aliases={9 + k: NY + 1 + k for k in range(NX)},
-        scratch_shapes=[pltpu.VMEM((NZ, 192, dl), BF)],
+        scratch_shapes=[pltpu.VMEM((NZ, 896, 128), BF)],
         compiler_params=params(6),
         cost_estimate=cost(0, 9_000_000),
     )(pick_at, *map(near, (pack, *gathered)), *map(far, cot_x))

time: 132 us -> 131 us (level)
  transfers between devices with their start and end apart: 39 -> 39, of which waited for: 19 -> 17; matrix products, arithmetic and copies ran while one was open for 1% -> 1% of each run, Pallas kernels for 15% -> 15%
where the time goes in v1:
time: 131 us; the launch traced here: 130 us
  starting transfers between devices  52.1 us (40%)
  waiting for transfers between devices  44.3 us (34%)
  Pallas kernels  29.7 us (23%)
  local copies, waits for them, and re-layouts  2.54 us (2%)
    ppermute x27, starting transfers between devices, deliver(): return lax.ppermute(value, axis, [(i, (i + k) % n) for i in range(n)])  41.8 us
    ppermute x27, waiting for transfers between devices, deliver(): return lax.ppermute(value, axis, [(i, (i + k) % n) for i in range(n)])  37.6 us
    ppermute x6, starting transfers between devices, ahead(): return lax.ppermute(value, axis, [(i, (i - k) % n) for i in range(n)])  9.58 us
    pallas_call x1, Pallas kernels, on_device(): pl.pallas_call(input_grad_kernel, out_shape=jax.ShapeDtypeStruct((rows, d...  6.94 us
    ppermute x6, waiting for transfers between devices, ahead(): return lax.ppermute(value, axis, [(i, (i - k) % n) for i in range(n)])  5.42 us
    pallas_call x1, Pallas kernels, on_device(): pl.pallas_call(kv_send_kernel, out_shape=half, in_specs=[SM] + [HB] * 5 +...  4.92 us
    pallas_call x1, Pallas kernels, on_device(): pl.pallas_call(kv_keep_kernel, out_shape=[made_far(rows, cl)] * NX, in_sp...  4.9 us
  transfers between devices with their start and end apart: 39, of which 17 were waited for; matrix products, arithmetic and copies ran while one was open for 1% of the time, Pallas kernels for 15%

profile of v1, /device:TPU:2, one launch (start us, length us, event | category | flops | bytes accessed | tf_op | source)
XLA Modules:
  0.0 130.5 jit_solution(12070154394132448720)
XLA Ops:
  3.7 4.0 %collective-permute-start.4 = (bf16[1216,128]{1,0:T(8,128)(2,1)S(1)}, bf16[1216,128]{1,0:T(8,128)(2,1)S(1)}, u32[]{:S(2)}, u32[]{:S(2)}) collective-permute-start(bf16[1216,128]{1,0:T(8,128)(2,1)S(1)} %shard_map.111._1.own), channel_id=1, source_target_pairs={{0,224},{32,0},{64,32},{96,64},{128,96},{160,128},{192,160},{224,1... | collective-permute-start | bytes 933896 | tf_op jit(solution)/shard_map/ppermute | solution.py:277
  7.7 7.3 %collective-permute-done.f1 = bf16[1216,128]{1,0:T(8,128)(2,1)S(1)} collective-permute-done((bf16[1216,128]{1,0:T(8,128)(2,1)S(1)}, bf16[1216,128]{1,0:T(8,128)(2,1)S(1)}, u32[]{:S(2)}, u32[]{:S(2)}) %collective-permute-start) | collective-permute-done | bytes 311328 | tf_op jit(solution)/shard_map/ppermute | solution.py:277
  19.6 2.2 %collective-permute-start.7 = (bf16[640,256]{1,0:T(8,128)(2,1)}, bf16[640,256]{1,0:T(8,128)(2,1)S(1)}, u32[]{:S(2)}, u32[]{:S(2)}) collective-permute-start(bf16[640,256]{1,0:T(8,128)(2,1)} %shard_map.112.refs_0_), channel_id=1, source_target_pairs={{0,6},{2,0},{4,2},{6,4},{1,7},{3,1},{5,3},{7,5},{8,14},{10,8},{12,... | collective-permute-start | bytes 983048 | tf_op jit(solution)/shard_map/ppermute | solution.py:273
  21.7 3.3 %collective-permute-start.5 = (bf16[1216,128]{1,0:T(8,128)(2,1)S(1)}, bf16[1216,128]{1,0:T(8,128)(2,1)S(1)}, u32[]{:S(2)}, u32[]{:S(2)}) collective-permute-start(bf16[1216,128]{1,0:T(8,128)(2,1)S(1)} %collective-permute-done.4.b1), channel_id=1, source_target_pairs={{0,224},{32,0},{64,32},{96,64},{128,96},{160,128},{192,160},{224,1... | collective-permute-start | bytes 933896 | tf_op jit(solution)/shard_map/ppermute | solution.py:277
  25.4 4.6 %collective-permute-done.5.b2 = bf16[1216,128]{1,0:T(8,128)(2,1)S(1)} collective-permute-done((bf16[1216,128]{1,0:T(8,128)(2,1)S(1)}, bf16[1216,128]{1,0:T(8,128)(2,1)S(1)}, u32[]{:S(2)}, u32[]{:S(2)}) %collective-permute-start.5) | collective-permute-done | bytes 311328 | tf_op jit(solution)/shard_map/ppermute | solution.py:277
  30.0 3.7 %collective-permute-start.6 = (bf16[1216,128]{1,0:T(8,128)(2,1)S(1)}, bf16[1216,128]{1,0:T(8,128)(2,1)S(1)}, u32[]{:S(2)}, u32[]{:S(2)}) collective-permute-start(bf16[1216,128]{1,0:T(8,128)(2,1)S(1)} %collective-permute-done.5.b2), channel_id=1, source_target_pairs={{0,224},{32,0},{64,32},{96,64},{128,96},{160,128},{192,160},{224,1... | collective-permute-start | bytes 933896 | tf_op jit(solution)/shard_map/ppermute | solution.py:277
  35.1 3.0 %collective-permute-done.6.b3 = bf16[1216,128]{1,0:T(8,128)(2,1)S(1)} collective-permute-done((bf16[1216,128]{1,0:T(8,128)(2,1)S(1)}, bf16[1216,128]{1,0:T(8,128)(2,1)S(1)}, u32[]{:S(2)}, u32[]{:S(2)}) %collective-permute-start.6) | collective-permute-done | bytes 311328 | tf_op jit(solution)/shard_map/ppermute | solution.py:277
  38.1 3.7 %collective-permute-done.3.f4 = bf16[1216,128]{1,0:T(8,128)(2,1)S(1)} collective-permute-done((bf16[1216,128]{1,0:T(8,128)(2,1)S(1)}, bf16[1216,128]{1,0:T(8,128)(2,1)S(1)}, u32[]{:S(2)}, u32[]{:S(2)}) %collective-permute-start.3) | collective-permute-done | bytes 311328 | tf_op jit(solution)/shard_map/ppermute | solution.py:277
  45.2 2.9 %collective-permute-start.12 = (bf16[96,896]{1,0:T(8,128)(2,1)S(1)}, bf16[96,896]{1,0:T(8,128)(2,1)S(1)}, u32[]{:S(2)}, u32[]{:S(2)}) collective-permute-start(bf16[96,896]{1,0:T(8,128)(2,1)S(1)} %get-tuple-element.37), channel_id=1, source_target_pairs={{0,16},{8,24},{16,0},{24,8},{1,17},{9,25},{17,1},{25,9},{2,18},{10... | collective-permute-start | bytes 516104 | tf_op jit(solution)/shard_map/ppermute | solution.py:277
  52.4 2.3 %collective-permute-start.11 = (bf16[8,64,640]{2,1,0:T(8,128)(2,1)}, bf16[8,64,640]{2,1,0:T(8,128)(2,1)}, u32[]{:S(2)}, u32[]{:S(2)}) collective-permute-start(bf16[8,64,640]{2,1,0:T(8,128)(2,1)} %shard_map.114.refs_0_), channel_id=1, source_target_pairs={{0,24},{8,0},{16,8},{24,16},{1,25},{9,1},{17,9},{25,17},{2,26},{10... | collective-permute-start | bytes 1966088 | tf_op jit(solution)/shard_map/ppermute | solution.py:277
  54.8 2.2 %collective-permute-done.12.a2 = bf16[96,896]{1,0:T(8,128)(2,1)S(1)} collective-permute-done((bf16[96,896]{1,0:T(8,128)(2,1)S(1)}, bf16[96,896]{1,0:T(8,128)(2,1)S(1)}, u32[]{:S(2)}, u32[]{:S(2)}) %collective-permute-start.12) | collective-permute-done | bytes 172064 | tf_op jit(solution)/shard_map/ppermute | solution.py:277
  64.2 3.4 %collective-permute-done.16.p2 = bf16[64,640]{1,0:T(8,128)(2,1)S(1)} collective-permute-done((bf16[64,640]{1,0:T(8,128)(2,1)S(1)}, bf16[64,640]{1,0:T(8,128)(2,1)S(1)}, u32[]{:S(2)}, u32[]{:S(2)}) %collective-permute-start.16) | collective-permute-done | bytes 81952 | tf_op jit(solution)/shard_map/ppermute | solution.py:273
  74.3 3.2 %collective-permute-start.20 = (bf16[4,64,640]{2,1,0:T(8,128)(2,1)}, bf16[4,64,640]{2,1,0:T(8,128)(2,1)S(1)}, u32[]{:S(2)}, u32[]{:S(2)}) collective-permute-start(bf16[4,64,640]{2,1,0:T(8,128)(2,1)} %get-tuple-element.46), channel_id=1, source_target_pairs={{0,24},{8,0},{16,8},{24,16},{1,25},{9,1},{17,9},{25,17},{2,26},{10... | collective-permute-start | bytes 983048 | tf_op jit(solution)/shard_map/ppermute | solution.py:277
  79.7 3.3 %collective-permute-done.24.b2 = bf16[96,896]{1,0:T(8,128)(2,1)S(1)} collective-permute-done((bf16[96,896]{1,0:T(8,128)(2,1)S(1)}, bf16[96,896]{1,0:T(8,128)(2,1)S(1)}, u32[]{:S(2)}, u32[]{:S(2)}) %collective-permute-start.24) | collective-permute-done | bytes 172064 | tf_op jit(solution)/shard_map/ppermute | solution.py:277
  83.0 2.5 %collective-permute-done.22.f2 = bf16[96,896]{1,0:T(8,128)(2,1)S(1)} collective-permute-done((bf16[96,896]{1,0:T(8,128)(2,1)S(1)}, bf16[96,896]{1,0:T(8,128)(2,1)S(1)}, u32[]{:S(2)}, u32[]{:S(2)}) %collective-permute-start.22) | collective-permute-done | bytes 172064 | tf_op jit(solution)/shard_map/ppermute | solution.py:277
  87.0 4.9 %shard_map.118 = bf16[4,640,256]{2,1,0:T(8,128)(2,1)} custom-call(s32[8]{0:T(128)S(1)} %and_select_fusion.12.at_ref, bf16[8,64,640]{2,1,0:T(8,128)(2,1)} %shard_map.114.refs_0_, bf16[8,64,640]{2,1,0:T(8,128)(2,1)} %collective-permute-done.11.next_ref.refs_1_, bf16[4,64,640]{2,1,0:T(8,128)(2,1)} %copy-done.4, bf16[4,64,640]{2,1,0:T(8,128)(2,1)} %copy-done.5, ...), custom_call_target="tpu_custom_call" | custom-call | flops 1000 | bytes 1000 | tf_op jit(solution)/shard_map/pallas_call | solution.py:412
  95.0 3.8 %collective-permute-done.35.b3 = bf16[96,896]{1,0:T(8,128)(2,1)S(1)} collective-permute-done((bf16[96,896]{1,0:T(8,128)(2,1)S(1)}, bf16[96,896]{1,0:T(8,128)(2,1)S(1)}, u32[]{:S(2)}, u32[]{:S(2)}) %collective-permute-start.35) | collective-permute-done | bytes 172064 | tf_op jit(solution)/shard_map/ppermute | solution.py:277
  100.7 4.9 %shard_map.119 = (bf16[640,256]{1,0:T(8,128)(2,1)}, bf16[640,256]{1,0:T(8,128)(2,1)}, bf16[640,256]{1,0:T(8,128)(2,1)}, bf16[640,256]{1,0:T(8,128)(2,1)}) custom-call(s32[8]{0:T(128)S(1)} %and_select_fusion.12.at_ref, bf16[8,64,640]{2,1,0:T(8,128)(2,1)} %shard_map.114.refs_0_, bf16[8,64,640]{2,1,0:T(8,128)(2,1)} %collective-permute-done.11.next_ref.refs_1_, ...), custom_call_target="tpu_custom_call" | custom-call | flops 1000 | bytes 1000 | tf_op jit(solution)/shard_map/pallas_call | solution.py:422
  105.7 2.6 %collective-permute-done.34.f4 = bf16[96,896]{1,0:T(8,128)(2,1)S(1)} collective-permute-done((bf16[96,896]{1,0:T(8,128)(2,1)S(1)}, bf16[96,896]{1,0:T(8,128)(2,1)S(1)}, u32[]{:S(2)}, u32[]{:S(2)}) %collective-permute-start.34) | collective-permute-done | bytes 172064 | tf_op jit(solution)/shard_map/ppermute | solution.py:277
  110.1 2.2 %collective-permute-start.27 = (bf16[640,256]{1,0:T(8,128)(2,1)S(1)}, bf16[640,256]{1,0:T(8,128)(2,1)S(1)}, u32[]{:S(2)}, u32[]{:S(2)}) collective-permute-start(bf16[640,256]{1,0:T(8,128)(2,1)S(1)} %copy-done.16), channel_id=1, source_target_pairs={{0,4},{2,6},{4,0},{6,2},{1,5},{3,7},{5,1},{7,3},{8,12},{10,14},{12... | collective-permute-start | bytes 983048 | tf_op jit(solution)/shard_map/ppermute | solution.py:277
  112.3 2.4 %collective-permute-start.28 = (bf16[640,256]{1,0:T(8,128)(2,1)S(1)}, bf16[640,256]{1,0:T(8,128)(2,1)S(1)}, u32[]{:S(2)}, u32[]{:S(2)}) collective-permute-start(bf16[640,256]{1,0:T(8,128)(2,1)S(1)} %copy-done.15), channel_id=1, source_target_pairs={{0,6},{2,0},{4,2},{6,4},{1,7},{3,1},{5,3},{7,5},{8,14},{10,8},{12,... | collective-permute-start | bytes 983048 | tf_op jit(solution)/shard_map/ppermute | solution.py:277
  114.7 2.9 %collective-permute-start.37 = (bf16[128,896]{1,0:T(8,128)(2,1)S(1)}, bf16[128,896]{1,0:T(8,128)(2,1)S(1)}, u32[]{:S(2)}, u32[]{:S(2)}) collective-permute-start(bf16[128,896]{1,0:T(8,128)(2,1)S(1)} %get-tuple-element.60), channel_id=1, source_target_pairs={{0,16},{8,24},{16,0},{24,8},{1,17},{9,25},{17,1},{25,9},{2,18},{10... | collective-permute-start | bytes 688136 | tf_op jit(solution)/shard_map/ppermute | solution.py:277
  119.6 6.9 %shard_map.121 = bf16[640,640]{1,0:T(8,128)(2,1)} custom-call(s32[8]{0:T(128)S(1)} %and_select_fusion.12.at_ref, bf16[8,64,640]{2,1,0:T(8,128)(2,1)} %shard_map.114.refs_0_, bf16[8,64,640]{2,1,0:T(8,128)(2,1)} %collective-permute-done.11.next_ref.refs_1_, bf16[4,64,640]{2,1,0:T(8,128)(2,1)} %copy-done.4, bf16[4,64,640]{2,1,0:T(8,128)(2,1)} %copy-done.5, ...), custom_call_target="tpu_custom_call" | custom-call | flops 1000 | bytes 1000 | tf_op jit(solution)/shard_map/pallas_call | solution.py:433
  128.2 2.3 %shard_map.120 = bf16[640,256]{1,0:T(8,128)(2,1)} custom-call(s32[1]{0:T(128)} %bitcast.yi_ref, bf16[640,256]{1,0:T(8,128)(2,1)} %get-tuple-element.47.p0._1, bf16[640,256]{1,0:T(8,128)(2,1)S(1)} %collective-permute-done.26.p1, bf16[640,256]{1,0:T(8,128)(2,1)S(1)} %collective-permute-done.27.p2, bf16[640,256]{1,0:T(8,128)(2,1)S(1)} %collective-permute-done.28.p3, ...), custom_call_target="tpu_custom_call" | custom-call | flops 167772160 | bytes 2000000 | tf_op jit(solution)/shard_map/pallas_call | solution.py:447
  (124 shorter events, 45.2 us)
Async XLA Ops:
  1.7 13.3 %collective-permute-start = (bf16[1216,128]{1,0:T(8,128)(2,1)S(1)}, bf16[1216,128]{1,0:T(8,128)(2,1)S(1)}, u32[]{:S(2)}, u32[]{:S(2)}) collective-permute-start(bf16[1216,128]{1,0:T(8,128)(2,1)S(1)} %shard_map.111._1.own), channel_id=1, source_target_pairs={{0,32},{32,64},{64,96},{96,128},{128,160},{160,192},{192,224},{224... | collective-permute-start | bytes 933896 | tf_op jit(solution)/shard_map/ppermute | solution.py:277
  3.7 18.0 %collective-permute-start.4 = (bf16[1216,128]{1,0:T(8,128)(2,1)S(1)}, bf16[1216,128]{1,0:T(8,128)(2,1)S(1)}, u32[]{:S(2)}, u32[]{:S(2)}) collective-permute-start(bf16[1216,128]{1,0:T(8,128)(2,1)S(1)} %shard_map.111._1.own), channel_id=1, source_target_pairs={{0,224},{32,0},{64,32},{96,64},{128,96},{160,128},{192,160},{224,1... | collective-permute-start | bytes 933896 | tf_op jit(solution)/shard_map/ppermute | solution.py:277
  15.0 10.0 %collective-permute-start.1 = (bf16[1216,128]{1,0:T(8,128)(2,1)S(1)}, bf16[1216,128]{1,0:T(8,128)(2,1)S(1)}, u32[]{:S(2)}, u32[]{:S(2)}) collective-permute-start(bf16[1216,128]{1,0:T(8,128)(2,1)S(1)} %collective-permute-done.f1), channel_id=1, source_target_pairs={{0,32},{32,64},{64,96},{96,128},{128,160},{160,192},{192,224},{224... | collective-permute-start | bytes 933896 | tf_op jit(solution)/shard_map/ppermute | solution.py:277
  16.9 16.9 %collective-permute-start.9 = (bf16[640,256]{1,0:T(8,128)(2,1)}, bf16[640,256]{1,0:T(8,128)(2,1)S(1)}, u32[]{:S(2)}, u32[]{:S(2)}) collective-permute-start(bf16[640,256]{1,0:T(8,128)(2,1)} %shard_map.112.refs_0_), channel_id=1, source_target_pairs={{0,2},{2,4},{4,6},{6,0},{1,3},{3,5},{5,7},{7,1},{8,10},{10,12},{12... | collective-permute-start | bytes 983048 | tf_op jit(solution)/shard_map/ppermute | solution.py:273
  18.4 15.5 %collective-permute-start.8 = (bf16[640,256]{1,0:T(8,128)(2,1)}, bf16[640,256]{1,0:T(8,128)(2,1)S(1)}, u32[]{:S(2)}, u32[]{:S(2)}) collective-permute-start(bf16[640,256]{1,0:T(8,128)(2,1)} %shard_map.112.refs_0_), channel_id=1, source_target_pairs={{0,4},{2,6},{4,0},{6,2},{1,5},{3,7},{5,1},{7,3},{8,12},{10,14},{12... | collective-permute-start | bytes 983048 | tf_op jit(solution)/shard_map/ppermute | solution.py:273
  19.6 15.6 %collective-permute-start.7 = (bf16[640,256]{1,0:T(8,128)(2,1)}, bf16[640,256]{1,0:T(8,128)(2,1)S(1)}, u32[]{:S(2)}, u32[]{:S(2)}) collective-permute-start(bf16[640,256]{1,0:T(8,128)(2,1)} %shard_map.112.refs_0_), channel_id=1, source_target_pairs={{0,6},{2,0},{4,2},{6,4},{1,7},{3,1},{5,3},{7,5},{8,14},{10,8},{12,... | collective-permute-start | bytes 983048 | tf_op jit(solution)/shard_map/ppermute | solution.py:273
  25.0 8.6 %collective-permute-start.2 = (bf16[1216,128]{1,0:T(8,128)(2,1)S(1)}, bf16[1216,128]{1,0:T(8,128)(2,1)S(1)}, u32[]{:S(2)}, u32[]{:S(2)}) collective-permute-start(bf16[1216,128]{1,0:T(8,128)(2,1)S(1)} %collective-permute-done.1.f2), channel_id=1, source_target_pairs={{0,32},{32,64},{64,96},{96,128},{128,160},{160,192},{192,224},{224... | collective-permute-start | bytes 933896 | tf_op jit(solution)/shard_map/ppermute | solution.py:277
  45.2 11.8 %collective-permute-start.12 = (bf16[96,896]{1,0:T(8,128)(2,1)S(1)}, bf16[96,896]{1,0:T(8,128)(2,1)S(1)}, u32[]{:S(2)}, u32[]{:S(2)}) collective-permute-start(bf16[96,896]{1,0:T(8,128)(2,1)S(1)} %get-tuple-element.37), channel_id=1, source_target_pairs={{0,16},{8,24},{16,0},{24,8},{1,17},{9,25},{17,1},{25,9},{2,18},{10... | collective-permute-start | bytes 516104 | tf_op jit(solution)/shard_map/ppermute | solution.py:277
  48.1 8.9 %collective-permute-start.13 = (bf16[96,896]{1,0:T(8,128)(2,1)S(1)}, bf16[96,896]{1,0:T(8,128)(2,1)S(1)}, u32[]{:S(2)}, u32[]{:S(2)}) collective-permute-start(bf16[96,896]{1,0:T(8,128)(2,1)S(1)} %get-tuple-element.38), channel_id=1, source_target_pairs={{0,24},{8,0},{16,8},{24,16},{1,25},{9,1},{17,9},{25,17},{2,26},{10... | collective-permute-start | bytes 516104 | tf_op jit(solution)/shard_map/ppermute | solution.py:277
  51.5 20.0 %collective-permute-start.18 = (bf16[8,64,640]{2,1,0:T(8,128)(2,1)}, bf16[8,64,640]{2,1,0:T(8,128)(2,1)S(1)}, u32[]{:S(2)}, u32[]{:S(2)}) collective-permute-start(bf16[8,64,640]{2,1,0:T(8,128)(2,1)} %shard_map.114.refs_0_), channel_id=1, source_target_pairs={{0,8},{8,16},{16,24},{24,0},{1,9},{9,17},{17,25},{25,1},{2,10},{10... | collective-permute-start | bytes 1966088 | tf_op jit(solution)/shard_map/ppermute | solution.py:277
  52.4 19.0 %collective-permute-start.11 = (bf16[8,64,640]{2,1,0:T(8,128)(2,1)}, bf16[8,64,640]{2,1,0:T(8,128)(2,1)}, u32[]{:S(2)}, u32[]{:S(2)}) collective-permute-start(bf16[8,64,640]{2,1,0:T(8,128)(2,1)} %shard_map.114.refs_0_), channel_id=1, source_target_pairs={{0,24},{8,0},{16,8},{24,16},{1,25},{9,1},{17,9},{25,17},{2,26},{10... | collective-permute-start | bytes 1966088 | tf_op jit(solution)/shard_map/ppermute | solution.py:277
  69.4 9.4 %collective-permute-start.21 = (bf16[96,896]{1,0:T(8,128)(2,1)S(1)}, bf16[96,896]{1,0:T(8,128)(2,1)S(1)}, u32[]{:S(2)}, u32[]{:S(2)}) collective-permute-start(bf16[96,896]{1,0:T(8,128)(2,1)S(1)} %get-tuple-element.40._1.own), channel_id=1, source_target_pairs={{0,32},{32,64},{64,96},{96,128},{128,160},{160,192},{192,224},{224... | collective-permute-start | bytes 516104 | tf_op jit(solution)/shard_map/ppermute | solution.py:277
  74.2 11.3 %collective-permute-start.19 = (bf16[4,64,640]{2,1,0:T(8,128)(2,1)}, bf16[4,64,640]{2,1,0:T(8,128)(2,1)S(1)}, u32[]{:S(2)}, u32[]{:S(2)}) collective-permute-start(bf16[4,64,640]{2,1,0:T(8,128)(2,1)} %get-tuple-element.45), channel_id=1, source_target_pairs={{0,8},{8,16},{16,24},{24,0},{1,9},{9,17},{17,25},{25,1},{2,10},{10... | collective-permute-start | bytes 983048 | tf_op jit(solution)/shard_map/ppermute | solution.py:277
  74.3 11.2 %collective-permute-start.20 = (bf16[4,64,640]{2,1,0:T(8,128)(2,1)}, bf16[4,64,640]{2,1,0:T(8,128)(2,1)S(1)}, u32[]{:S(2)}, u32[]{:S(2)}) collective-permute-start(bf16[4,64,640]{2,1,0:T(8,128)(2,1)} %get-tuple-element.46), channel_id=1, source_target_pairs={{0,24},{8,0},{16,8},{24,16},{1,25},{9,1},{17,9},{25,17},{2,26},{10... | collective-permute-start | bytes 983048 | tf_op jit(solution)/shard_map/ppermute | solution.py:277
  94.4 15.6 %collective-permute-start.29 = (bf16[640,256]{1,0:T(8,128)(2,1)S(1)}, bf16[640,256]{1,0:T(8,128)(2,1)S(1)}, u32[]{:S(2)}, u32[]{:S(2)}) collective-permute-start(bf16[640,256]{1,0:T(8,128)(2,1)S(1)} %copy-done.3), channel_id=1, source_target_pairs={{0,1},{1,0},{2,3},{3,2},{4,5},{5,4},{6,7},{7,6},{8,9},{9,8},{10,11... | collective-permute-start | bytes 983048 | tf_op jit(solution)/shard_map/ppermute | solution.py:408
  94.5 15.6 %collective-permute-start.30 = (bf16[640,256]{1,0:T(8,128)(2,1)}, bf16[640,256]{1,0:T(8,128)(2,1)S(1)}, u32[]{:S(2)}, u32[]{:S(2)}) collective-permute-start(bf16[640,256]{1,0:T(8,128)(2,1)} %get-tuple-element.54.refs_6_), channel_id=1, source_target_pairs={{0,1},{1,0},{2,3},{3,2},{4,5},{5,4},{6,7},{7,6},{8,9},{9,8},{10,11... | collective-permute-start | bytes 983048 | tf_op jit(solution)/shard_map/ppermute | solution.py:408
  98.8 13.5 %collective-permute-start.31 = (bf16[640,256]{1,0:T(8,128)(2,1)}, bf16[640,256]{1,0:T(8,128)(2,1)S(1)}, u32[]{:S(2)}, u32[]{:S(2)}) collective-permute-start(bf16[640,256]{1,0:T(8,128)(2,1)} %get-tuple-element.55.refs_7_), channel_id=1, source_target_pairs={{0,1},{1,0},{2,3},{3,2},{4,5},{5,4},{6,7},{7,6},{8,9},{9,8},{10,11... | collective-permute-start | bytes 983048 | tf_op jit(solution)/shard_map/ppermute | solution.py:408
  100.2 14.5 %collective-permute-start.32 = (bf16[640,256]{1,0:T(8,128)(2,1)S(1)}, bf16[640,256]{1,0:T(8,128)(2,1)S(1)}, u32[]{:S(2)}, u32[]{:S(2)}) collective-permute-start(bf16[640,256]{1,0:T(8,128)(2,1)S(1)} %copy-done.7), channel_id=1, source_target_pairs={{0,1},{1,0},{2,3},{3,2},{4,5},{5,4},{6,7},{7,6},{8,9},{9,8},{10,11... | collective-permute-start | bytes 983048 | tf_op jit(solution)/shard_map/ppermute | solution.py:408
  109.3 8.8 %collective-permute-start.36 = (bf16[128,896]{1,0:T(8,128)(2,1)S(1)}, bf16[128,896]{1,0:T(8,128)(2,1)S(1)}, u32[]{:S(2)}, u32[]{:S(2)}) collective-permute-start(bf16[128,896]{1,0:T(8,128)(2,1)S(1)} %get-tuple-element.59), channel_id=1, source_target_pairs={{0,8},{8,16},{16,24},{24,0},{1,9},{9,17},{17,25},{25,1},{2,10},{10... | collective-permute-start | bytes 688136 | tf_op jit(solution)/shard_map/ppermute | solution.py:277
  110.0 18.2 %collective-permute-start.26 = (bf16[640,256]{1,0:T(8,128)(2,1)S(1)}, bf16[640,256]{1,0:T(8,128)(2,1)S(1)}, u32[]{:S(2)}, u32[]{:S(2)}) collective-permute-start(bf16[640,256]{1,0:T(8,128)(2,1)S(1)} %copy-done.17), channel_id=1, source_target_pairs={{0,2},{2,4},{4,6},{6,0},{1,3},{3,5},{5,7},{7,1},{8,10},{10,12},{12... | collective-permute-start | bytes 983048 | tf_op jit(solution)/shard_map/ppermute | solution.py:277
  110.1 18.1 %collective-permute-start.27 = (bf16[640,256]{1,0:T(8,128)(2,1)S(1)}, bf16[640,256]{1,0:T(8,128)(2,1)S(1)}, u32[]{:S(2)}, u32[]{:S(2)}) collective-permute-start(bf16[640,256]{1,0:T(8,128)(2,1)S(1)} %copy-done.16), channel_id=1, source_target_pairs={{0,4},{2,6},{4,0},{6,2},{1,5},{3,7},{5,1},{7,3},{8,12},{10,14},{12... | collective-permute-start | bytes 983048 | tf_op jit(solution)/shard_map/ppermute | solution.py:277
  112.3 15.8 %collective-permute-start.28 = (bf16[640,256]{1,0:T(8,128)(2,1)S(1)}, bf16[640,256]{1,0:T(8,128)(2,1)S(1)}, u32[]{:S(2)}, u32[]{:S(2)}) collective-permute-start(bf16[640,256]{1,0:T(8,128)(2,1)S(1)} %copy-done.15), channel_id=1, source_target_pairs={{0,6},{2,0},{4,2},{6,4},{1,7},{3,1},{5,3},{7,5},{8,14},{10,8},{12,... | collective-permute-start | bytes 983048 | tf_op jit(solution)/shard_map/ppermute | solution.py:277
  114.7 11.8 %collective-permute-start.37 = (bf16[128,896]{1,0:T(8,128)(2,1)S(1)}, bf16[128,896]{1,0:T(8,128)(2,1)S(1)}, u32[]{:S(2)}, u32[]{:S(2)}) collective-permute-start(bf16[128,896]{1,0:T(8,128)(2,1)S(1)} %get-tuple-element.60), channel_id=1, source_target_pairs={{0,16},{8,24},{16,0},{24,8},{1,17},{9,25},{17,1},{25,9},{2,18},{10... | collective-permute-start | bytes 688136 | tf_op jit(solution)/shard_map/ppermute | solution.py:277
  118.1 9.2 %collective-permute-start.38 = (bf16[128,896]{1,0:T(8,128)(2,1)S(1)}, bf16[128,896]{1,0:T(8,128)(2,1)S(1)}, u32[]{:S(2)}, u32[]{:S(2)}) collective-permute-start(bf16[128,896]{1,0:T(8,128)(2,1)S(1)} %get-tuple-element.61), channel_id=1, source_target_pairs={{0,24},{8,0},{16,8},{24,16},{1,25},{9,1},{17,9},{25,17},{2,26},{10... | collective-permute-start | bytes 688136 | tf_op jit(solution)/shard_map/ppermute | solution.py:277
  (35 other events, 280.1 us)
